TPU v7x, 512 devices: a whole 4x8x8 slice. The times are simulated.
512 devices in a mesh: region: 64 (over y_lo, z, core), member: 8 (over y_hi, x).
Axes of the slice: x: 4, y: 8 (y_hi: 2, y_lo: 4; y = y_hi * 4 + y_lo), z: 8, core: 2. Of those that a mesh axis runs over, the one named last changes fastest.
Arguments:
- prior_state: float32 [80, 15, 16384], P('member', None, 'region'), may hold values from -6 to 6
- observed: float32 [4, 32768], P(None, 'region'), may hold values from -8 to 8
- obs_error: float32 [4, 32768], P(None, 'region'), may hold values from 1.5 to 6
- obs_index: int32 [4, 32768], P(None, 'region'), may hold values from 0 to 3839
- pattern: int32 [4, 64, 3, 4, 2], P(None, 'region'), may hold values 0 or 1
- ancestors: int32 [4, 64, 80], P(None, 'region'), may hold values from 0 to 79
Outputs:
- posterior: float32 [80, 15, 16384], P('member', None, 'region')
All inputs are finite; a program needn't handle non-finite values. No bound on the sum of `pattern` on one device may be relied on, other than what follows from the above.
Results may differ from a plain program's by a relative error of at most 0.0003.
Values sent between devices are 32-bit elements; how exact they have to be, the bound alone decides.
A program may use at most 64 MiB of HBM per device.

v0:
```python
import jax
import jax.numpy as jnp
from jax import lax
from jax.sharding import PartitionSpec as P

BATCHES = 4
TILE = 128


def with_halo(cells, sides, width):
    for axis, dim in sides:
        count = lax.axis_size(axis)
        head = lax.slice_in_dim(cells, 0, width, axis=dim)
        tail = lax.slice_in_dim(cells, cells.shape[dim] - width, cells.shape[dim], axis=dim)
        cells = jnp.concatenate(
            [
                lax.ppermute(tail, axis, [(i, (i + 1) % count) for i in range(count)]),
                cells,
                lax.ppermute(head, axis, [((i + 1) % count, i) for i in range(count)]),
            ],
            axis=dim,
        )
    return cells


def taper_piece(pattern_k, neighbor, obs_count, cell_count, column_ids):
    within = jnp.arange(obs_count, dtype=jnp.int32)
    offset = (neighbor - 1) * cell_count + within * cell_count // obs_count
    distance = jnp.abs(offset[:, None] - column_ids[None, :]).astype(jnp.float32)
    taper = jnp.exp(-distance / (0.5 * cell_count))
    row_blocks = jnp.repeat(pattern_k.astype(jnp.float32), TILE, axis=0)
    tile_ids = jnp.arange(pattern_k.shape[1], dtype=jnp.int32)
    column_onehot = (column_ids[:, None] // TILE == tile_ids[None, :]).astype(jnp.float32)
    blocks = jnp.dot(
        row_blocks,
        column_onehot.T,
        precision=lax.Precision.HIGHEST,
        preferred_element_type=jnp.float32,
    )
    return taper * blocks


def local_scores(nearby, pattern_batch, obs_count, cell_count, column_ids):
    total = jnp.zeros((nearby.shape[0], column_ids.shape[0]), jnp.float32)
    for neighbor in range(3):
        piece = lax.slice_in_dim(nearby, neighbor * obs_count, (neighbor + 1) * obs_count, axis=1)
        loc_weights = taper_piece(
            pattern_batch[neighbor], neighbor, obs_count, cell_count, column_ids
        )
        total = total + jnp.dot(
            piece, loc_weights, precision=lax.Precision.HIGHEST, preferred_element_type=jnp.float32
        )
    return total


def likelihood_terms(values, observed_row, error_row):
    misfit = observed_row[None, :] - values
    return -(misfit * misfit) * (0.5 / (error_row * error_row))[None, :]


def local(prior_state, observed, obs_error, obs_index, pattern, ancestors):
    group_size, var_count, cell_count = prior_state.shape
    obs_count = observed.shape[1]
    member_pos = lax.axis_index("member")
    column_ids = jnp.arange(cell_count, dtype=jnp.int32)
    state = prior_state
    for batch in range(BATCHES):
        flat = state.reshape(group_size, var_count * cell_count)
        values = jnp.take(flat, obs_index[batch], axis=1)
        terms = likelihood_terms(values, observed[batch], obs_error[batch])
        nearby = with_halo(terms, (("region", 1),), obs_count)
        scores = local_scores(nearby, pattern[batch, 0], obs_count, cell_count, column_ids)
        highest = lax.pmax(jnp.max(scores, axis=0), "member")
        raised = jnp.exp(scores - highest[None, :])
        weighted = jnp.einsum("mc,mvc->vc", raised, state, precision=lax.Precision.HIGHEST)
        weight_sum, weighted_sum = lax.psum((jnp.sum(raised, axis=0), weighted), "member")
        post_mean = weighted_sum / weight_sum[None, :]
        whole = lax.all_gather(state, "member", axis=0, tiled=True)
        own_parents = lax.dynamic_slice_in_dim(
            ancestors[batch, 0], member_pos * group_size, group_size, 0
        )
        chosen = jnp.take(whole, own_parents, axis=0)
        centre = post_mean[None]
        state = centre + 0.8 * (chosen - centre) + 0.3 * (state - centre)
    return state


def solution(mesh):
    placed = (
        P("member", None, "region"),
        P(None, "region"),
        P(None, "region"),
        P(None, "region"),
        P(None, "region", None, None, None),
        P(None, "region", None),
    )
    return jax.shard_map(
        local, mesh=mesh, in_specs=placed, out_specs=P("member", None, "region"), check_vma=False
    )
```

profile of v0, /device:TPU:32, one launch (start us, length us, event | category | flops | bytes accessed | tf_op | source)
XLA Modules:
  0.0 419.0 jit_solution(9109841860899087263)
XLA Ops:
  7.3 1.5 copy.39
  11.5 10.7 %collective-permute-start.1 = (f32[10,512]{0,1:T(8,128)S(1)}, f32[10,512]{0,1:T(8,128)S(1)}, u32[]{:S(2)}, u32[]{:S(2)}) collective-permute-start(f32[10,512]{0,1:T(8,128)S(1)} %fusion.27), channel_id=1, source_target_pairs={{8,0},{16,8},{24,16},{32,24},{40,32},{48,40},{56,48},{64,56},{72,6... | collective-permute-start | bytes 61448 | tf_op jit(solution)/shard_map/ppermute | solution.py:19
  22.2 1.9 collective-permute-start
  28.7 1.3 fusion.7
  36.4 1.5 fusion.70
  38.0 29.0 %pmax.28 = f32[256]{0:T(256)S(1)} all-reduce(f32[256]{0:T(256)S(1)} %get-tuple-element.59), channel_id=1, replica_groups=mesh['region'=64,'member'=8] {'member'}, use_global_device_ids=true, to_apply=%region_1.3 | all-reduce | flops 256 | bytes 2048 | tf_op jit(solution)/shard_map/pmax | solution.py:73
  67.0 48.2 %all-reduce.3 = (f32[15,256]{1,0:T(8,128)S(1)}, f32[256]{0:T(256)S(1)}) all-reduce(f32[15,256]{1,0:T(8,128)S(1)} %bitcast.224, f32[256]{0:T(256)S(1)} %get-tuple-element.29), channel_id=1, replica_groups=mesh['region'=64,'member'=8] {'member'}, use_global_device_ids=true, to_apply=%region_2.4 | all-reduce | flops 4096 | bytes 32768 | tf_op jit(solution)/shard_map/psum | solution.py:76
  115.3 1.9 gather_fusion.1
  118.6 1.3 fusion.3
  123.3 1.9 collective-permute-start.3
  125.2 2.4 collective-permute-start.2
  127.6 1.6 fusion.76
  129.8 10.6 %collective-permute-done.2 = f32[10,512]{0,1:T(8,128)S(1)} collective-permute-done((f32[10,512]{0,1:T(8,128)S(1)}, f32[10,512]{0,1:T(8,128)S(1)}, u32[]{:S(2)}, u32[]{:S(2)}) %collective-permute-start.2) | collective-permute-done | bytes 20512 | tf_op jit(solution)/shard_map/ppermute | solution.py:17
  141.0 24.9 %pmax.29 = f32[256]{0:T(256)S(1)} all-reduce(f32[256]{0:T(256)S(1)} %get-tuple-element.61), channel_id=1, replica_groups=mesh['region'=64,'member'=8] {'member'}, use_global_device_ids=true, to_apply=%region_6.9 | all-reduce | flops 256 | bytes 2048 | tf_op jit(solution)/shard_map/pmax | solution.py:73
  166.0 48.4 %all-reduce.2 = (f32[15,256]{1,0:T(8,128)S(1)}, f32[256]{0:T(256)S(1)}) all-reduce(f32[15,256]{1,0:T(8,128)S(1)} %bitcast.225, f32[256]{0:T(256)S(1)} %get-tuple-element.27), channel_id=1, replica_groups=mesh['region'=64,'member'=8] {'member'}, use_global_device_ids=true, to_apply=%region_7.10 | all-reduce | flops 4096 | bytes 32768 | tf_op jit(solution)/shard_map/psum | solution.py:76
  214.4 2.0 gather_fusion.3
  218.1 1.3 fusion
  221.4 1.9 collective-permute-start.5
  223.4 2.4 collective-permute-start.4
  225.8 1.6 fusion.78
  228.0 9.2 %collective-permute-done.4 = f32[10,512]{0,1:T(8,128)S(1)} collective-permute-done((f32[10,512]{0,1:T(8,128)S(1)}, f32[10,512]{0,1:T(8,128)S(1)}, u32[]{:S(2)}, u32[]{:S(2)}) %collective-permute-start.4) | collective-permute-done | bytes 20512 | tf_op jit(solution)/shard_map/ppermute | solution.py:17
  237.8 25.6 %pmax.30 = f32[256]{0:T(256)S(1)} all-reduce(f32[256]{0:T(256)S(1)} %get-tuple-element.63), channel_id=1, replica_groups=mesh['region'=64,'member'=8] {'member'}, use_global_device_ids=true, to_apply=%region_11.14 | all-reduce | flops 256 | bytes 2048 | tf_op jit(solution)/shard_map/pmax | solution.py:73
  263.4 49.5 %all-reduce.1 = (f32[15,256]{1,0:T(8,128)S(1)}, f32[256]{0:T(256)S(1)}) all-reduce(f32[15,256]{1,0:T(8,128)S(1)} %bitcast.226, f32[256]{0:T(256)S(1)} %get-tuple-element.25), channel_id=1, replica_groups=mesh['region'=64,'member'=8] {'member'}, use_global_device_ids=true, to_apply=%region_12.15 | all-reduce | flops 4096 | bytes 32768 | tf_op jit(solution)/shard_map/psum | solution.py:76
  312.9 2.0 gather_fusion.5
  315.8 1.3 fusion.1
  319.7 1.9 collective-permute-start.7
  321.6 2.4 collective-permute-start.6
  324.0 1.6 fusion.80
  326.2 8.3 %collective-permute-done.6 = f32[10,512]{0,1:T(8,128)S(1)} collective-permute-done((f32[10,512]{0,1:T(8,128)S(1)}, f32[10,512]{0,1:T(8,128)S(1)}, u32[]{:S(2)}, u32[]{:S(2)}) %collective-permute-start.6) | collective-permute-done | bytes 20512 | tf_op jit(solution)/shard_map/ppermute | solution.py:17
  335.1 25.2 %pmax.31 = f32[256]{0:T(256)S(1)} all-reduce(f32[256]{0:T(256)S(1)} %get-tuple-element.65), channel_id=1, replica_groups=mesh['region'=64,'member'=8] {'member'}, use_global_device_ids=true, to_apply=%region_16.19 | all-reduce | flops 256 | bytes 2048 | tf_op jit(solution)/shard_map/pmax | solution.py:73
  360.3 49.4 %all-reduce = (f32[15,256]{1,0:T(8,128)S(1)}, f32[256]{0:T(256)S(1)}) all-reduce(f32[15,256]{1,0:T(8,128)S(1)} %bitcast.227, f32[256]{0:T(256)S(1)} %get-tuple-element.23), channel_id=1, replica_groups=mesh['region'=64,'member'=8] {'member'}, use_global_device_ids=true, to_apply=%region_17.20 | all-reduce | flops 4096 | bytes 32768 | tf_op jit(solution)/shard_map/psum | solution.py:76
  409.8 1.9 gather_fusion.7
  (181 shorter events, 30.1 us)
Async XLA Ops:
  6.5 18.8 %copy-start.25 = (s32[4,1,80]{2,1,0:T(1,128)S(1)}, s32[4,1,80]{2,1,0:T(1,128)}, u32[]{:S(2)}) copy-start(s32[4,1,80]{2,1,0:T(1,128)} %param.15) | copy-start | bytes 3844
  6.5 18.9 %copy-start.6 = (s32[4,1,3,4,2]{3,4,2,1,0:T(2,128)S(1)}, s32[4,1,3,4,2]{3,4,2,1,0:T(2,128)}, u32[]{:S(2)}) copy-start(s32[4,1,3,4,2]{3,4,2,1,0:T(2,128)} %param.14) | copy-start | bytes 1156
  6.5 108.7 %all-gather.5.cloned.1.call-start = ((), (), s32[]{:S(2)}) async-start(), calls=%async_computation | async-start | bytes 1474560 | tf_op jit(solution)/shard_map/all_gather | solution.py:78
  7.3 207.2 %all-gather.7.cloned.1.call-start = ((), (), s32[]{:S(2)}) async-start(), calls=%async_computation.1 | async-start | bytes 1474560 | tf_op jit(solution)/shard_map/all_gather | solution.py:78
  11.5 24.4 %collective-permute-start.1 = (f32[10,512]{0,1:T(8,128)S(1)}, f32[10,512]{0,1:T(8,128)S(1)}, u32[]{:S(2)}, u32[]{:S(2)}) collective-permute-start(f32[10,512]{0,1:T(8,128)S(1)} %fusion.27), channel_id=1, source_target_pairs={{8,0},{16,8},{24,16},{32,24},{40,32},{48,40},{56,48},{64,56},{72,6... | collective-permute-start | bytes 61448 | tf_op jit(solution)/shard_map/ppermute | solution.py:19
  22.2 14.2 %collective-permute-start = (f32[10,512]{0,1:T(8,128)S(1)}, f32[10,512]{0,1:T(8,128)}, u32[]{:S(2)}, u32[]{:S(2)}) collective-permute-start(f32[10,512]{0,1:T(8,128)S(1)} %fusion.27), channel_id=1, source_target_pairs={{0,8},{8,16},{16,24},{24,32},{32,40},{40,48},{48,56},{56,64},{64,7... | collective-permute-start | bytes 61448 | tf_op jit(solution)/shard_map/ppermute | solution.py:17
  24.2 94.4 %copy-start.28 = (s32[512]{0:T(512)}, s32[512]{0:T(512)S(1)}, u32[]{:S(2)}) copy-start(s32[512]{0:T(512)S(1)} %broadcast_add_fusion.1) | copy-start | bytes 6148
  24.2 95.8 %copy-start.32 = (s32[256]{0:T(256)}, s32[256]{0:T(256)S(1)}, u32[]{:S(2)}) copy-start(s32[256]{0:T(256)S(1)} %and_select_fusion) | copy-start | bytes 3076
  24.2 95.8 %copy-start.26 = (s32[512]{0:T(512)}, s32[512]{0:T(512)S(1)}, u32[]{:S(2)}) copy-start(s32[512]{0:T(512)S(1)} %add_select_fusion) | copy-start | bytes 6148
  33.1 33.9 %copy-start.3 = (f32[10,15,256]{2,1,0:T(8,128)S(1)}, f32[10,15,256]{2,1,0:T(8,128)}, u32[]{:S(2)}) copy-start(f32[10,15,256]{2,1,0:T(8,128)} %param.10) | copy-start | bytes 460804
  117.9 195.0 %all-gather.9.cloned.1.call-start = ((), (), s32[]{:S(2)}) async-start(), calls=%async_computation.2 | async-start | bytes 1474560 | tf_op jit(solution)/shard_map/all_gather | solution.py:78
  118.6 4.3 %copy-start.13 = (f32[1,512]{1,0:T(1,128)S(1)}, f32[1,512]{1,0:T(1,128)}, u32[]{:S(2)}) copy-start(f32[1,512]{1,0:T(1,128)} %get-tuple-element.48) | copy-start | bytes 6148
  118.6 4.3 %copy-start.14 = (f32[1,512]{1,0:T(1,128)S(1)}, f32[1,512]{1,0:T(1,128)}, u32[]{:S(2)}) copy-start(f32[1,512]{1,0:T(1,128)} %get-tuple-element.44) | copy-start | bytes 6148
  121.9 94.6 %copy-start.24 = (pred[10]{0:T(512)(128)(4,1)S(1)}, pred[10]{0:T(512)(128)(4,1)}, u32[]{:S(2)}) copy-start(pred[10]{0:T(512)(128)(4,1)} %get-tuple-element.19) | copy-start | bytes 34
  123.3 94.2 %copy-start.8 = (f32[4,2]{1,0:T(4,128)S(1)}, f32[4,2]{1,0:T(4,128)}, u32[]{:S(2)}) copy-start(f32[4,2]{1,0:T(4,128)} %copy.48) | copy-start | bytes 100
  123.3 94.3 %copy-start.31 = (s32[512]{0:T(512)S(1)}, s32[512]{0:T(512)}, u32[]{:S(2)}) copy-start(s32[512]{0:T(512)} %copy-done.30) | copy-start | bytes 6148
  123.3 94.3 %copy-start.33 = (s32[256]{0:T(256)S(1)}, s32[256]{0:T(256)}, u32[]{:S(2)}) copy-start(s32[256]{0:T(256)} %copy-done.32) | copy-start | bytes 3076
  123.3 6.0 %collective-permute-start.3 = (f32[10,512]{0,1:T(8,128)S(1)}, f32[10,512]{0,1:T(8,128)S(1)}, u32[]{:S(2)}, u32[]{:S(2)}) collective-permute-start(f32[10,512]{0,1:T(8,128)S(1)} %fusion.24), channel_id=1, source_target_pairs={{8,0},{16,8},{24,16},{32,24},{40,32},{48,40},{56,48},{64,56},{72,6... | collective-permute-start | bytes 61448 | tf_op jit(solution)/shard_map/ppermute | solution.py:19
  125.2 15.2 %collective-permute-start.2 = (f32[10,512]{0,1:T(8,128)S(1)}, f32[10,512]{0,1:T(8,128)S(1)}, u32[]{:S(2)}, u32[]{:S(2)}) collective-permute-start(f32[10,512]{0,1:T(8,128)S(1)} %fusion.24), channel_id=1, source_target_pairs={{0,8},{8,16},{16,24},{24,32},{32,40},{40,48},{48,56},{56,64},{64,7... | collective-permute-start | bytes 61448 | tf_op jit(solution)/shard_map/ppermute | solution.py:17
  129.2 88.8 %copy-start.7 = (f32[4,2]{1,0:T(4,128)S(1)}, f32[4,2]{1,0:T(4,128)}, u32[]{:S(2)}) copy-start(f32[4,2]{1,0:T(4,128)} %copy.54) | copy-start | bytes 100
  129.2 88.9 %copy-start.29 = (s32[512]{0:T(512)S(1)}, s32[512]{0:T(512)}, u32[]{:S(2)}) copy-start(s32[512]{0:T(512)} %copy-done.28) | copy-start | bytes 6148
  217.3 192.5 %all-gather.11.cloned.1.call-start = ((), (), s32[]{:S(2)}) async-start(), calls=%async_computation.3 | async-start | bytes 1474560 | tf_op jit(solution)/shard_map/all_gather | solution.py:78
  219.4 8.0 %copy-start.4 = (f32[512,256]{0,1:T(8,128)S(1)}, f32[512,256]{0,1:T(8,128)}, u32[]{:S(2)}) copy-start(f32[512,256]{0,1:T(8,128)} %fusion.3) | copy-start | bytes 1572868
  220.1 94.9 %copy-start.22 = (pred[10]{0:T(512)(128)(4,1)S(1)}, pred[10]{0:T(512)(128)(4,1)}, u32[]{:S(2)}) copy-start(pred[10]{0:T(512)(128)(4,1)} %get-tuple-element.17) | copy-start | bytes 34
  221.4 94.3 %copy-start.15 = (s32[512]{0:T(512)S(1)}, s32[512]{0:T(512)}, u32[]{:S(2)}) copy-start(s32[512]{0:T(512)} %compare_select_fusion) | copy-start | bytes 6148
  221.4 94.4 %copy-start.27 = (s32[512]{0:T(512)S(1)}, s32[512]{0:T(512)}, u32[]{:S(2)}) copy-start(s32[512]{0:T(512)} %copy-done.26) | copy-start | bytes 6148
  221.4 5.9 %collective-permute-start.5 = (f32[10,512]{0,1:T(8,128)S(1)}, f32[10,512]{0,1:T(8,128)S(1)}, u32[]{:S(2)}, u32[]{:S(2)}) collective-permute-start(f32[10,512]{0,1:T(8,128)S(1)} %fusion.21), channel_id=1, source_target_pairs={{8,0},{16,8},{24,16},{32,24},{40,32},{48,40},{56,48},{64,56},{72,6... | collective-permute-start | bytes 61448 | tf_op jit(solution)/shard_map/ppermute | solution.py:19
  223.4 13.8 %collective-permute-start.4 = (f32[10,512]{0,1:T(8,128)S(1)}, f32[10,512]{0,1:T(8,128)S(1)}, u32[]{:S(2)}, u32[]{:S(2)}) collective-permute-start(f32[10,512]{0,1:T(8,128)S(1)} %fusion.21), channel_id=1, source_target_pairs={{0,8},{8,16},{16,24},{24,32},{32,40},{40,48},{48,56},{56,64},{64,7... | collective-permute-start | bytes 61448 | tf_op jit(solution)/shard_map/ppermute | solution.py:17
  317.7 8.0 %copy-start.5 = (f32[512,256]{0,1:T(8,128)S(1)}, f32[512,256]{0,1:T(8,128)}, u32[]{:S(2)}) copy-start(f32[512,256]{0,1:T(8,128)} %fusion) | copy-start | bytes 1572868
  318.3 93.4 %copy-start.23 = (pred[10]{0:T(512)(128)(4,1)S(1)}, pred[10]{0:T(512)(128)(4,1)}, u32[]{:S(2)}) copy-start(pred[10]{0:T(512)(128)(4,1)} %get-tuple-element.15) | copy-start | bytes 34
  319.7 6.0 %collective-permute-start.7 = (f32[10,512]{0,1:T(8,128)S(1)}, f32[10,512]{0,1:T(8,128)S(1)}, u32[]{:S(2)}, u32[]{:S(2)}) collective-permute-start(f32[10,512]{0,1:T(8,128)S(1)} %fusion.18), channel_id=1, source_target_pairs={{8,0},{16,8},{24,16},{32,24},{40,32},{48,40},{56,48},{64,56},{72,6... | collective-permute-start | bytes 61448 | tf_op jit(solution)/shard_map/ppermute | solution.py:19
  321.6 13.0 %collective-permute-start.6 = (f32[10,512]{0,1:T(8,128)S(1)}, f32[10,512]{0,1:T(8,128)S(1)}, u32[]{:S(2)}, u32[]{:S(2)}) collective-permute-start(f32[10,512]{0,1:T(8,128)S(1)} %fusion.18), channel_id=1, source_target_pairs={{0,8},{8,16},{16,24},{24,32},{32,40},{40,48},{48,56},{56,64},{64,7... | collective-permute-start | bytes 61448 | tf_op jit(solution)/shard_map/ppermute | solution.py:17
  (14 other events, 42.2 us)
Sparse Core Ops, SparseCore 0:
  10.6 66.9 all-gather.4
  118.0 58.3 all-gather.6
  217.4 57.7 all-gather.8
  315.9 56.2 all-gather.10
where the time goes:
time: 420 us; the launch traced here: 419 us
  blocking collectives  300 us (71%)
  waiting for transfers between devices  28.9 us (7%)
  starting transfers between devices  26 us (6%)
  matrix products  20.8 us (5%)
  local copies, waits for them, and re-layouts  18.5 us (4%)
  between operations  14.1 us (3%)
  other arithmetic  10.5 us (2%)
    psum x4, blocking collectives, local(): lax.psum((jnp.sum(raised, axis=0), weighted), 'member')  196 us
    pmax x4, blocking collectives, local(): highest = lax.pmax(jnp.max(scores, axis=0), 'member')  105 us
    ppermute x4, waiting for transfers between devices, with_halo(): lax.ppermute(tail, axis, [(i, (i + 1) % count) for i in range(count)])  28.2 us
    ppermute x4, starting transfers between devices, with_halo(): lax.ppermute(head, axis, [((i + 1) % count, i) for i in range(count)])  16.5 us
    dot_general x12, matrix products, local_scores(): jnp.dot(piece, loc_weights, precision=lax.Precision.HIGHEST, preferred_el...  10.9 us
    dot_general x12, matrix products, taper_piece(): jnp.dot(row_blocks, column_onehot.T, precision=lax.Precision.HIGHEST, pre...  9.91 us
    ppermute x4, starting transfers between devices, with_halo(): lax.ppermute(tail, axis, [(i, (i + 1) % count) for i in range(count)])  9.14 us
  transfers between devices with their start and end apart: 12, of which 3 were waited for; matrix products, arithmetic and copies ran while one was open for 9% of the time, Pallas kernels for 0%

commit v1 on v0

v1 whole, which is shorter than its diff:
```python
import functools

import jax
import jax.numpy as jnp
from jax import lax
from jax.experimental import pallas as pl
from jax.experimental.pallas import tpu as pltpu
from jax.sharding import PartitionSpec as P

MESH = pl.DeviceIdType.MESH
F32, BF16 = jnp.float32, jnp.bfloat16

BATCHES = 4
MEMBERS = 80
GROUP = 8
OWN = 10
VARS = 15
CELLS = 256
OBS = 512
OTILES = 4
ALONG_X = 4
LEFT, RIGHT, SELF = 0, 1, 2


def split2(a):
    hi = a.astype(BF16)
    lo = (a - hi.astype(F32)).astype(BF16)
    return hi, lo


def split3(a):
    hi = a.astype(BF16)
    rest = a - hi.astype(F32)
    mid = rest.astype(BF16)
    lo = (rest - mid.astype(F32)).astype(BF16)
    return hi, mid, lo


def dot(a, b):
    return jnp.dot(a, b, preferred_element_type=F32)


def body(
    regions,
    x_ref, obs_ref, err_ref, idx_ref, pat_ref, anc_ref,
    out_ref,
    xs, xh, lhs, onehot, own_h, ha, hb, ya, yb0, yb1, ha3, hb3, yb03, yb13, xa, xb,
    taper, loc_hi, loc_lo, pe, pe_in, halo_out, halo_in, self_scores, w_all, mean_h, mean_x,
    send, recv,
):
    r = lax.axis_index("region")
    me = lax.axis_index("member")
    along_x = me % ALONG_X
    far = (me + ALONG_X) % GROUP
    base = me - along_x
    far_base = far - along_x

    def beside(step):
        n = r + step
        wrapped = jnp.logical_or(n < 0, n >= regions)
        m = jnp.where(wrapped, far, me)
        return ((n + regions) % regions, m)

    left, right = beside(-1), beside(1)
    partners = [(r, base + (along_x + d) % ALONG_X) for d in (1, 2, 3)]
    across = (r, far)

    def copy(src, dst, sem, device):
        return pltpu.make_async_remote_copy(
            src_ref=src, dst_ref=dst, send_sem=send.at[sem], recv_sem=recv.at[sem],
            device_id=device, device_id_type=MESH,
        )

    barrier = pltpu.get_barrier_semaphore()
    for device in (*partners, across, left, right):
        pl.semaphore_signal(barrier, inc=1, device_id=device, device_id_type=MESH)

    xs[...] = jnp.zeros_like(xs)
    xh[...] = jnp.zeros_like(xh)
    for m in range(OWN):
        x = x_ref[m]
        xs[m, pl.ds(0, VARS), :] = x
        for half in (0, 1):
            xh[half, pl.ds(16 * m, VARS), :] = x[:, 128 * half : 128 * half + 128]
    for v in range(VARS):
        x = jnp.concatenate([xh[half, pl.ds(v, 16, stride=16), :] for half in (0, 1)], axis=1)
        for part, piece in enumerate(split3(x)):
            lhs[pl.ds(part * 16 * VARS + 16 * v, 16), :] = piece

    def sample(b):
        where = idx_ref[pl.ds(b, 1), :]
        var, cell = where // CELLS, where % CELLS
        rows = lax.broadcasted_iota(jnp.int32, (CELLS, OBS), 0)
        onehot[b] = jnp.where(rows == cell, 1.0, 0.0).astype(BF16)
        got = dot(lhs[...], onehot[b])
        n = 16 * VARS
        got = got[:n] + got[n : 2 * n] + got[2 * n :]
        total = jnp.zeros((16, OBS), F32)
        for v in range(VARS):
            total = total + jnp.where(var == v, got[16 * v : 16 * v + 16], 0.0)
        for t in range(OTILES):
            own_h[b // 2, pl.ds(4 * (b % 2) + t, 16, stride=8), :] = total[:, 128 * t : 128 * t + 128]

    def rows_of(member):
        return pl.ds(pl.multiple_of(member * (8 * OWN), 8), 8 * OWN)

    def members_of(member):
        return pl.ds(member * OWN, OWN)

    def gather(src, dst, mine, theirs, sem):
        near = [copy(src, dst.at[mine], sem + i, p) for i, p in enumerate(partners)]
        over = copy(src, dst.at[mine], sem + 3, across)
        block = dst.at[theirs]
        onward = [copy(block, block, sem + 4 + i, p) for i, p in enumerate(partners)]
        return near, over, onward

    sample(0)
    sample(1)
    for b in range(BATCHES):
        for k in range(3):
            p = pat_ref[b, 0, k].astype(F32)
            lane = lax.broadcasted_iota(jnp.int32, (OTILES, CELLS), 1)
            pe[k, pl.ds(4 * b, 4), :] = jnp.where(lane < 128, p[:, 0:1], p[:, 1:2])

    pl.semaphore_wait(barrier, 6)

    gather_a = gather(own_h.at[0, pl.ds(0, 8 * OWN)], ha, rows_of(me), rows_of(far), 0)
    gather_a[1].start()
    for c in gather_a[0]:
        c.start()
    pattern_copies = [
        copy(pe.at[0], pe_in.at[1], 21, left),
        copy(pe.at[2], pe_in.at[0], 22, right),
    ]
    for c in pattern_copies:
        c.start()
    ha[rows_of(me), :] = own_h[0, pl.ds(0, 8 * OWN), :]

    sample(2)
    sample(3)
    gather_b = gather(own_h.at[1, pl.ds(0, 8 * OWN)], hb, rows_of(me), rows_of(far), 7)
    gather_b[1].start()
    for c in gather_b[0]:
        c.start()
    hb[rows_of(me), :] = own_h[1, pl.ds(0, 8 * OWN), :]
    gather_x = gather(xs, xa, members_of(me), members_of(far), 14)
    gather_x[1].start()
    for c in gather_x[0]:
        c.start()
    xa[members_of(me)] = xs[...]

    at = lax.broadcasted_iota(jnp.int32, (OBS, CELLS), 0) // 2
    column = lax.broadcasted_iota(jnp.int32, (OBS, CELLS), 1)
    for dest, shift in ((LEFT, CELLS), (RIGHT, -CELLS), (SELF, 0)):
        distance = jnp.abs(at + shift - column).astype(F32)
        taper[:, CELLS * dest : CELLS * (dest + 1)] = jnp.exp(distance * (-1.0 / (0.5 * CELLS)))

    def localize(b):
        for dest in (LEFT, RIGHT, SELF):
            for t in range(OTILES):
                k = 4 * b + t
                row = pe[1, pl.ds(k, 1), :] if dest == SELF else pe_in[dest, pl.ds(k, 1), :]
                block = (pl.ds(128 * t, 128), pl.ds(CELLS * dest, CELLS))
                loc_hi[block], loc_lo[block] = split2(taper[block] * row)

    for c in pattern_copies:
        c.wait()
    localize(0)

    gather_a[1].wait()
    for c in gather_a[2]:
        c.start()
    for c in (*gather_a[0], *gather_a[2]):
        c.wait()

    y_of = [(ha, hb), (ya, yb0), (None, yb1), (None, yb0)]

    def rows_at(b, batch):
        y = y_of[b][batch // 2]
        return [y[pl.ds(4 * (batch % 2) + t, MEMBERS, stride=8), :] for t in range(OTILES)]

    def terms(b):
        tiles = []
        for t, y in enumerate(rows_at(b, b)):
            lanes = pl.ds(128 * t, 128)
            if b > 0:
                y = y - 0.1 * mean_h[pl.ds(4 * b + t, 1), :]
            miss = obs_ref[pl.ds(b, 1), lanes] - y
            err = err_ref[pl.ds(b, 1), lanes]
            tiles.append(-(miss * miss) * (0.5 / (err * err)))
        return jnp.concatenate(tiles, axis=1)

    def spread(q_hi, q_lo, cols):
        both = dot(jnp.concatenate([q_hi, q_lo], axis=0), loc_hi[:, cols])
        return both[:MEMBERS] + both[MEMBERS:] + dot(q_hi, loc_lo[:, cols])

    def stack(src, dst):
        def step(m, _):
            dst[m] = src[pl.ds(pl.multiple_of(m * 8, 8), 8), :]
            return 0

        lax.fori_loop(0, MEMBERS, step, 0, unroll=8)

    def evolve(b, src, dst, dst3, half):
        old = None if b == 0 else 0.11 * mean_h[pl.ds(8 * half, 8), :]

        def step(m, _):
            y = 0.8 * src[anc_ref[b, 0, m]] + 0.3 * src[m]
            y = y if old is None else y - old
            dst[pl.ds(pl.multiple_of(m * 8, 8), 8), :] = y
            if dst3 is not None:
                dst3[m] = y
            return 0

        lax.fori_loop(0, MEMBERS, step, 0, unroll=8)

    def mean_at(b, batch, w_parts):
        wm = dot(w_parts, onehot[batch])
        wm = wm[:MEMBERS] + wm[MEMBERS:]
        found = []
        for t, y in enumerate(rows_at(b, batch)):
            m = jnp.sum(wm[:, 128 * t : 128 * t + 128] * y, axis=0, keepdims=True)
            if b > 0:
                m = m - 0.1 * mean_h[pl.ds(4 * batch + t, 1), :]
            found.append(m)
        return found

    def store_mean(batch, found):
        for t, m in enumerate(found):
            mean_h[pl.ds(4 * batch + t, 1), :] = m

    def mean_state(b, x):
        def step(m, acc):
            w = w_all[b, pl.ds(m, 1), :]
            return acc + w * x[m]

        return lax.fori_loop(0, MEMBERS, step, jnp.zeros((16, CELLS), F32), unroll=8)

    def advance(b, x, y):
        mean_x[...] = 0.1 * mean_state(b, x)

        def step(m, _):
            y[m] = 0.8 * x[anc_ref[b, 0, m]] + 0.3 * x[m] - mean_x[...]
            return 0

        lax.fori_loop(0, MEMBERS, step, 0, unroll=8)

    w_parts = None
    for b in range(BATCHES):
        q_hi, q_lo = split2(terms(b))
        halo = []
        for dest, device in ((LEFT, left), (RIGHT, right)):
            halo_out[b, dest] = spread(q_hi, q_lo, pl.ds(CELLS * dest, CELLS))
            c = copy(halo_out.at[b, dest], halo_in.at[b, 1 - dest], 23 + 2 * b + dest, device)
            c.start()
            halo.append(c)
        self_scores[...] = spread(q_hi, q_lo, pl.ds(CELLS * SELF, CELLS))

        if b == 0:
            gather_b[1].wait()
            for c in gather_b[2]:
                c.start()
            for c in (*gather_b[0], *gather_b[2]):
                c.wait()
            stack(ha, ha3)
            stack(hb, hb3)
            evolve(0, ha3, ya, None, 0)
            evolve(0, hb3, yb0, yb03, 1)
        if b == 1:
            for batch in (2, 3):
                store_mean(batch, mean_at(0, batch, w_parts))
            evolve(1, yb03, yb1, yb13, 1)
            gather_x[1].wait()
            for c in gather_x[2]:
                c.start()
        if b == 2:
            store_mean(3, mean_at(1, 3, w_parts))
            evolve(2, yb13, yb0, None, 1)
            for c in (*gather_x[0], *gather_x[2]):
                c.wait()
            advance(0, xa, xb)
        if b == 3:
            advance(1, xb, xa)
            advance(2, xa, xb)
        if b + 1 < BATCHES:
            localize(b + 1)

        for c in halo:
            c.wait()
        scores = self_scores[...] + halo_in[b, 0] + halo_in[b, 1]
        raised = jnp.exp(scores - jnp.max(scores, axis=0, keepdims=True))
        weights = raised / jnp.sum(raised, axis=0, keepdims=True)
        w_all[b] = weights
        if b + 1 < BATCHES:
            w_parts = jnp.concatenate(split2(weights), axis=0)
            store_mean(b + 1, mean_at(b, b + 1, w_parts))

    mean = 0.1 * mean_state(BATCHES - 1, xb)
    for i in range(OWN):
        m = me * OWN + i
        x = 0.8 * xb[anc_ref[BATCHES - 1, 0, m]] + 0.3 * xb[m] - mean
        out_ref[i] = x[:VARS]


def local(regions, *args):
    whole = pl.BlockSpec(memory_space=pltpu.VMEM)
    vmem = pltpu.VMEM
    return pl.pallas_call(
        functools.partial(body, regions),
        out_shape=jax.ShapeDtypeStruct((OWN, VARS, CELLS), F32),
        in_specs=[whole] * 5 + [pl.BlockSpec(memory_space=pltpu.SMEM)],
        out_specs=whole,
        scratch_shapes=[
            vmem((OWN, 16, CELLS), F32),
            vmem((2, 256, 128), F32),
            vmem((3 * 16 * VARS, CELLS), BF16),
            vmem((BATCHES, CELLS, OBS), BF16),
            vmem((2, 128, 128), F32),
            vmem((8 * MEMBERS, 128), F32),
            vmem((8 * MEMBERS, 128), F32),
            vmem((8 * MEMBERS, 128), F32),
            vmem((8 * MEMBERS, 128), F32),
            vmem((8 * MEMBERS, 128), F32),
            vmem((MEMBERS, 8, 128), F32),
            vmem((MEMBERS, 8, 128), F32),
            vmem((MEMBERS, 8, 128), F32),
            vmem((MEMBERS, 8, 128), F32),
            vmem((MEMBERS, 16, CELLS), F32),
            vmem((MEMBERS, 16, CELLS), F32),
            vmem((OBS, 3 * CELLS), F32),
            vmem((OBS, 3 * CELLS), BF16),
            vmem((OBS, 3 * CELLS), BF16),
            vmem((3, 4 * BATCHES, CELLS), F32),
            vmem((2, 4 * BATCHES, CELLS), F32),
            vmem((BATCHES, 2, MEMBERS, CELLS), F32),
            vmem((BATCHES, 2, MEMBERS, CELLS), F32),
            vmem((MEMBERS, CELLS), F32),
            vmem((BATCHES, MEMBERS, CELLS), F32),
            vmem((16, 128), F32),
            vmem((16, CELLS), F32),
            pltpu.SemaphoreType.DMA((31,)),
            pltpu.SemaphoreType.DMA((31,)),
        ],
        compiler_params=pltpu.CompilerParams(
            collective_id=0, has_side_effects=True, vmem_limit_bytes=48 << 20
        ),
        name="particle_filter",
    )(*args)


def solution(mesh):
    placed = (
        P("member", None, "region"),
        P(None, "region"),
        P(None, "region"),
        P(None, "region"),
        P(None, "region", None, None, None),
        P(None, "region", None),
    )
    return jax.shard_map(
        functools.partial(local, mesh.shape["region"]),
        mesh=mesh, in_specs=placed, out_specs=P("member", None, "region"), check_vma=False,
    )
```

time: 420 us -> 52.3 us (0.12)
  the two profiles are of different devices: /device:TPU:32 before, /device:TPU:2 now
where the time goes in v1:
time: 52.3 us; the launch traced here: 52.1 us
  Pallas kernels  49.6 us (95%)
  local copies, waits for them, and re-layouts  2.5 us (5%)
    pallas_call x1, Pallas kernels, local(): pl.pallas_call(functools.partial(body, regions), out_shape=jax.ShapeDtype...  49.6 us
    unnamed x12, local copies, waits for them, and re-layouts  2.5 us

profile of v1, /device:TPU:2, one launch (start us, length us, event | category | flops | bytes accessed | tf_op | source)
XLA Modules:
  0.0 52.1 jit_solution(14732823278467673037)
XLA Ops:
  0.0 0.0 copy-start.4
  0.0 0.0 copy-start.3
  0.0 0.0 copy-start.2
  0.0 0.0 copy-start.1
  0.0 0.9 %copy.7.pat_ref = s32[4,1,3,4,2]{4,3,2,1,0:T(4,128)S(1)} copy(s32[4,1,3,4,2]{3,4,2,1,0:T(2,128)} %param.10) | data formatting | bytes 768 | tf_op args[4]
  0.9 0.0 copy-done.4
  0.9 0.0 copy-done.3
  0.9 0.0 copy-done.2
  0.9 0.0 copy-done.1
  0.9 0.0 copy-start
  1.0 0.9 %copy-done = f32[10,15,256]{2,1,0:T(8,128)S(1)} copy-done((f32[10,15,256]{2,1,0:T(8,128)S(1)}, f32[10,15,256]{2,1,0:T(8,128)}, u32[]{:S(2)}) %copy-start) | copy-done | bytes 153624
  1.9 49.6 %particle_filter.1 = f32[10,15,256]{2,1,0:T(8,128)S(1)} custom-call(f32[10,15,256]{2,1,0:T(8,128)S(1)} %copy-done, f32[4,512]{1,0:T(4,128)S(1)} %copy-done.1, f32[4,512]{1,0:T(4,128)S(1)} %copy-done.2, s32[4,512]{1,0:T(4,128)S(1)} %copy-done.3, s32[4,1,3,4,2]{4,3,2,1,0:T(4,128)S(1)} %copy.7.pat_ref, s32[4,1,80]{2,1,0:T(1,128)S(1)} %copy-done.4), custom_call_target="tpu_custom_call" | custom-call | tf_op jit(solution)/shard_map/particle_filter/pallas_call | solution.py:308
  51.4 0.7 %copy.9 = f32[10,15,256]{2,1,0:T(8,128)} copy(f32[10,15,256]{2,1,0:T(8,128)S(1)} %particle_filter.1) | data formatting | bytes 307200
Async XLA Ops:
  0.0 0.9 %copy-start.4 = (s32[4,1,80]{2,1,0:T(1,128)S(1)}, s32[4,1,80]{2,1,0:T(1,128)}, u32[]{:S(2)}) copy-start(s32[4,1,80]{2,1,0:T(1,128)} %anc_ref.1) | copy-start | bytes 3844
  0.0 0.9 %copy-start.3 = (s32[4,512]{1,0:T(4,128)S(1)}, s32[4,512]{1,0:T(4,128)}, u32[]{:S(2)}) copy-start(s32[4,512]{1,0:T(4,128)} %idx_ref.1) | copy-start | bytes 24580
  0.0 0.9 %copy-start.2 = (f32[4,512]{1,0:T(4,128)S(1)}, f32[4,512]{1,0:T(4,128)}, u32[]{:S(2)}) copy-start(f32[4,512]{1,0:T(4,128)} %err_ref.1) | copy-start | bytes 24580
  0.0 0.9 %copy-start.1 = (f32[4,512]{1,0:T(4,128)S(1)}, f32[4,512]{1,0:T(4,128)}, u32[]{:S(2)}) copy-start(f32[4,512]{1,0:T(4,128)} %obs_ref.1) | copy-start | bytes 24580
  0.9 0.9 %copy-start = (f32[10,15,256]{2,1,0:T(8,128)S(1)}, f32[10,15,256]{2,1,0:T(8,128)}, u32[]{:S(2)}) copy-start(f32[10,15,256]{2,1,0:T(8,128)} %x_ref.1) | copy-start | bytes 460804

commit v2 on v1

v2 whole, which is shorter than its diff:
```python
import functools

import jax
import jax.numpy as jnp
from jax import lax
from jax.experimental import pallas as pl
from jax.experimental.pallas import tpu as pltpu
from jax.sharding import PartitionSpec as P

MESH = pl.DeviceIdType.MESH
F32, BF16 = jnp.float32, jnp.bfloat16

BATCHES = 4
MEMBERS = 80
GROUP = 8
OWN = 10
VARS = 15
CELLS = 256
OBS = 512
OTILES = 4
ALONG_X = 4
Z_CHIPS, EARLY_FAR, EARLY_NEAR = 8, 4, 4


def split2(a):
    hi = a.astype(BF16)
    lo = (a - hi.astype(F32)).astype(BF16)
    return hi, lo


def split3(a):
    hi = a.astype(BF16)
    rest = a - hi.astype(F32)
    mid = rest.astype(BF16)
    lo = (rest - mid.astype(F32)).astype(BF16)
    return hi, mid, lo


def dot(a, b):
    return jnp.dot(a, b, preferred_element_type=F32)


def body(
    regions,
    x_hbm, obs_hbm, err_hbm, idx_hbm, pat_hbm, anc_hbm,
    out_ref,
    x_ref, obs_ref, err_ref, idx_ref, pat_ref, anc_ref,
    xs, xh, lhs, onehot, own_2d, own_h, y10, y20, y30, y11, y21, y31, y22, y32, y33,
    h1, h2, h3, h21, h31, h32, xa, xb,
    taper, loc_hi, loc_lo, reach, land, z_own, z_first, self_own, self_far, s_out, s_in, s_all, z_out, z_in,
    self_scores, w_all, mean_h, mean_x,
    load_sem, send, recv,
):
    r = lax.axis_index("region")
    me = lax.axis_index("member")
    along_x = me % ALONG_X
    far = (me + ALONG_X) % GROUP
    base = me - along_x
    near_half = me // ALONG_X
    z = (r // 2) % Z_CHIPS
    early_far, early_near = z < EARLY_FAR, z < EARLY_NEAR

    def beside(step):
        n = r + step
        wrapped = jnp.logical_or(n < 0, n >= regions)
        n = (n + regions) % regions
        return (n, jnp.where(wrapped, far, me)), (n, me), (n, far)

    (left, left_same, left_far), (right, right_same, right_far) = beside(-1), beside(1)
    partners = [(r, base + (along_x + d) % ALONG_X) for d in (1, 2, 3)]
    across = (r, far)

    def copy(src, dst, sem, device):
        return pltpu.make_async_remote_copy(
            src_ref=src, dst_ref=dst, send_sem=send.at[sem], recv_sem=recv.at[sem],
            device_id=device, device_id_type=MESH,
        )

    barrier = pltpu.get_barrier_semaphore()
    greeted = (across, left_same, right_same, left_far, right_far, *partners)
    for device in greeted:
        pl.semaphore_signal(barrier, inc=1, device_id=device, device_id_type=MESH)

    held = ((idx_hbm, idx_ref), (pat_hbm, pat_ref), (x_hbm, x_ref), (obs_hbm, obs_ref), (err_hbm, err_ref), (anc_hbm, anc_ref))
    loads = [pltpu.make_async_copy(src, dst, load_sem.at[i]) for i, (src, dst) in enumerate(held)]
    for c in loads:
        c.start()

    at = lax.broadcasted_iota(jnp.int32, (OBS, CELLS), 0) // 2
    column = lax.broadcasted_iota(jnp.int32, (OBS, CELLS), 1)
    taper[...] = jnp.exp(jnp.abs(at - column).astype(F32) * (-1.0 / (0.5 * CELLS)))
    at = lax.broadcasted_iota(jnp.int32, (OBS, 128), 0)
    tile = lax.broadcasted_iota(jnp.int32, (OBS, 128), 1)
    away = jnp.where(tile < OTILES, at // 2, CELLS - at // 2).astype(F32)
    held_by = jnp.logical_and(tile < 2 * OTILES, tile % OTILES == at // 128)
    reach[0], reach[1] = split2(jnp.where(held_by, jnp.exp(away * (-1.0 / (0.5 * CELLS))), 0.0))
    for zeroed in (xs, xh, land):
        zeroed[...] = jnp.zeros_like(zeroed)

    def locate(b):
        where = idx_ref[pl.ds(b, 1), :]
        rows = lax.broadcasted_iota(jnp.int32, (CELLS, OBS), 0)
        onehot[b] = jnp.where(rows == where % CELLS, 1.0, 0.0).astype(BF16)

    lane = lax.broadcasted_iota(jnp.int32, (1, CELLS), 1)

    def blocks(b, k, t):
        low, high = (pat_ref[b, 0, k, c, t].astype(F32) for c in (0, 1))
        return jnp.where(lane < 128, low, high)

    def localize(b):
        for t in range(OTILES):
            rows = pl.ds(128 * t, 128)
            loc_hi[rows, :], loc_lo[rows, :] = split2(taper[rows, :] * blocks(b, 1, t))
        lands = []
        for k, gap in ((2, CELLS - lane), (0, lane)):
            factor = jnp.exp(gap.astype(F32) * (-1.0 / (0.5 * CELLS)))
            lands += [factor * blocks(b, k, t) for t in range(OTILES)]
        hi, lo = split2(jnp.concatenate(lands + [jnp.zeros((8, CELLS), F32)], axis=0))
        land[b % 2, 0, pl.ds(0, 16), :], land[b % 2, 1, pl.ds(0, 16), :] = hi, lo

    def product(a, b_hi, b_lo):
        n = a.shape[0]
        hi, lo = split2(a)
        both = dot(jnp.concatenate([hi, lo], axis=0), b_hi)
        return both[:n] + both[n:] + dot(hi, b_lo)

    def own_scores(q):
        return product(q, loc_hi[...], loc_lo[...])

    def beside_sums(q):
        return product(q, reach[0], reach[1])

    def beside_scores(b, from_left, from_right):
        lanes = lax.broadcasted_iota(jnp.int32, from_left.shape, 1)
        return product(jnp.where(lanes < OTILES, from_right, from_left), land[b % 2, 0], land[b % 2, 1])

    loads[0].wait()
    locate(0)
    loads[1].wait()
    localize(0)
    loads[2].wait()
    for m in range(OWN):
        x = x_ref[m]
        xs[m, pl.ds(0, VARS), :] = x
        for half in (0, 1):
            xh[half, pl.ds(16 * m, VARS), :] = x[:, 128 * half : 128 * half + 128]
    for v in range(VARS):
        x = jnp.concatenate([xh[half, pl.ds(v, 16, stride=16), :] for half in (0, 1)], axis=1)
        for part, piece in enumerate(split3(x)):
            lhs[pl.ds(part * 16 * VARS + 16 * v, 16), :] = piece

    def sample(b):
        var = idx_ref[pl.ds(b, 1), :] // CELLS
        got = dot(lhs[...], onehot[b])
        n = 16 * VARS
        got = got[:n] + got[n : 2 * n] + got[2 * n :]
        total = jnp.zeros((16, OBS), F32)
        for v in range(VARS):
            total = total + jnp.where(var == v, got[16 * v : 16 * v + 16], 0.0)
        return total

    def keep_sample(b):
        total = sample(b)
        for t in range(OTILES):
            own_2d[b - 1, pl.ds(t, 16, stride=8), :] = total[:, 128 * t : 128 * t + 128]
        for m in range(OWN):
            own_h[b - 1, m] = own_2d[b - 1, pl.ds(8 * m, OTILES), :]

    def term(b, t, y):
        lanes = pl.ds(128 * t, 128)
        miss = obs_ref[pl.ds(b, 1), lanes] - y
        err = err_ref[pl.ds(b, 1), lanes]
        return -(miss * miss) * (0.5 / (err * err))

    def members_of(member):
        return pl.ds(member * OWN, OWN)

    def gather(src, dst, sem):
        mine, theirs = dst.at[members_of(me)], dst.at[members_of(far)]
        near = [copy(src, mine, sem + i, p) for i, p in enumerate(partners)]
        over = copy(src, mine, sem + 3, across)
        onward = [copy(theirs, theirs, sem + 4 + i, p) for i, p in enumerate(partners)]
        return near, over, onward

    def start(copies):
        for c in copies:
            c.start()

    def wait(copies):
        for c in copies:
            c.wait()

    for c in loads[3:]:
        c.wait()
    first = sample(0)
    q = jnp.concatenate([term(0, t, first[:, 128 * t : 128 * t + 128]) for t in range(OTILES)], axis=1)
    self_own[...] = own_scores(q)
    z_own[...] = beside_sums(q)

    pl.semaphore_wait(barrier, len(greeted))

    first_copies = [
        copy(self_own, self_far, 21, across),
        copy(z_own, z_first.at[1, 1], 22, left_far),
        copy(z_own, z_first.at[0, 1], 23, right_far),
        copy(z_own, z_first.at[1, 0], 24, left_same),
        copy(z_own, z_first.at[0, 0], 25, right_same),
    ]
    start(first_copies)

    held_h = {1: h1, 2: h2, 3: h3}
    samples = {b: gather(own_h.at[b - 1], held_h[b], 35 + 7 * (b - 1)) for b in (1, 2, 3)}
    members = gather(xs, xa, 0)
    for b in (1, 2, 3):
        locate(b)
        keep_sample(b)
        held_h[b][members_of(me)] = own_h[b - 1]
        if b < 3:
            samples[b][1].start()
        start(samples[b][0])

    @pl.when(early_far)
    def _():
        members[1].start()

    @pl.when(early_near)
    def _():
        start(members[0])

    xa[members_of(me)] = xs[...]

    y_of = {(0, 1): y10, (0, 2): y20, (0, 3): y30, (1, 1): y11, (1, 2): y21, (1, 3): y31, (2, 2): y22, (2, 3): y32, (3, 3): y33}
    blocks_of = {(0, 1): h1, (0, 2): h2, (0, 3): h3, (1, 2): h21, (1, 3): h31, (2, 3): h32}

    def rows_at(b, batch):
        return [y_of[b, batch][pl.ds(t, MEMBERS, stride=8), :] for t in range(OTILES)]

    def mean_rows(batch):
        return pl.ds(8 * (batch - 1), OTILES)

    def mean_row(batch, t):
        return pl.ds(8 * (batch - 1) + t, 1)

    def terms(b):
        return jnp.concatenate(
            [term(b, t, y - 0.1 * mean_h[mean_row(b, t), :]) for t, y in enumerate(rows_at(b, b))], axis=1
        )

    def evolve(b, batch):
        src, flat = blocks_of[b, batch], y_of[0, batch] if b == 0 else None
        rows, blocks = y_of[b + 1, batch], blocks_of.get((b + 1, batch))
        old = None if b == 0 else 0.11 * mean_h[mean_rows(batch), :]

        def step(m, _):
            at = pl.ds(pl.multiple_of(m * 8, 8), OTILES)
            now = src[m]
            y = 0.8 * src[anc_ref[b, 0, m]] + 0.3 * now
            y = y if old is None else y - old
            rows[at, :] = y
            if blocks is not None:
                blocks[m] = y
            if flat is not None:
                flat[at, :] = now
            return 0

        lax.fori_loop(0, MEMBERS, step, 0, unroll=8)

    def mean_at(b, batch, w_parts):
        wm = dot(w_parts, onehot[batch])
        wm = wm[:MEMBERS] + wm[MEMBERS:]
        for t, y in enumerate(rows_at(b, batch)):
            m = jnp.sum(wm[:, 128 * t : 128 * t + 128] * y, axis=0, keepdims=True)
            if b > 0:
                m = m - 0.1 * mean_h[mean_row(batch, t), :]
            mean_h[mean_row(batch, t), :] = m

    def mean_state(b, x):
        def step(m, acc):
            w = w_all[b, pl.ds(m, 1), :]
            return acc + w * x[m]

        return lax.fori_loop(0, MEMBERS, step, jnp.zeros((16, CELLS), F32), unroll=8)

    def advance(b, x, y):
        mean_x[...] = 0.1 * mean_state(b, x)

        def step(m, _):
            y[m] = 0.8 * x[anc_ref[b, 0, m]] + 0.3 * x[m] - mean_x[...]
            return 0

        lax.fori_loop(0, MEMBERS, step, 0, unroll=8)

    def weigh(b, scores):
        raised = jnp.exp(scores - jnp.max(scores, axis=0, keepdims=True))
        weights = raised / jnp.sum(raised, axis=0, keepdims=True)
        w_all[b] = weights
        return jnp.concatenate(split2(weights), axis=0)

    samples[1][1].wait()
    start(samples[1][2])
    wait(first_copies)
    samples[3][1].start()

    @pl.when(jnp.logical_not(early_far))
    def _():
        members[1].start()

    sums = beside_scores(
        0,
        jnp.concatenate([z_first[0, 0], z_first[0, 1]], axis=0),
        jnp.concatenate([z_first[1, 0], z_first[1, 1]], axis=0),
    )
    s_out[pl.ds(0, 16), :] = sums[:16] + self_own[...]
    s_out[pl.ds(OWN, OWN), :] = (sums[16:] + self_far[...])[:OWN]
    s_out[pl.ds(2 * OWN, 4), :] = jnp.zeros((4, CELLS), F32)
    s_copies = [copy(s_out, s_in.at[along_x], 26 + i, p) for i, p in enumerate(partners)]
    start(s_copies)
    s_in[along_x] = s_out[...]
    localize(1)
    samples[2][1].wait()
    start(samples[2][2])
    wait((*samples[1][0], *samples[1][2]))
    evolve(0, 1)
    wait(s_copies)
    for half, first in ((0, near_half), (1, 1 - near_half)):
        rows = jnp.concatenate([s_in[i, pl.ds(OWN * half, OWN), :] for i in range(ALONG_X)], axis=0)
        s_all[pl.ds(pl.multiple_of(first * (MEMBERS // 2), 8), MEMBERS // 2), :] = rows

    w_parts = weigh(0, s_all[...])
    mean_at(0, 1, w_parts)

    for b in range(1, BATCHES):
        q = terms(b)
        z_out[b - 1] = beside_sums(q)
        halo = [
            copy(z_out.at[b - 1], z_in.at[b - 1, 1], 27 + 2 * b, left),
            copy(z_out.at[b - 1], z_in.at[b - 1, 0], 28 + 2 * b, right),
        ]
        start(halo)
        self_scores[...] = own_scores(q)

        if b == 1:
            samples[3][1].wait()
            start(samples[3][2])

            @pl.when(jnp.logical_not(early_near))
            def _():
                start(members[0])

            @pl.when(early_far)
            def _():
                members[1].wait()
                start(members[2])

            wait((*samples[2][0], *samples[2][2]))
            evolve(0, 2)
            mean_at(0, 2, w_parts)
            evolve(1, 2)
            held_w = w_parts
        if b == 2:
            @pl.when(jnp.logical_not(early_far))
            def _():
                members[1].wait()
                start(members[2])

            wait((*samples[3][0], *samples[3][2]))
            evolve(0, 3)
            mean_at(0, 3, held_w)
            evolve(1, 3)
            mean_at(1, 3, w_parts)
            evolve(2, 3)
        if b == 3:
            wait((*members[0], *members[2]))
            advance(0, xa, xb)
            advance(1, xb, xa)
            advance(2, xa, xb)
        if b + 1 < BATCHES:
            localize(b + 1)

        wait(halo)
        w_parts = weigh(b, self_scores[...] + beside_scores(b, z_in[b - 1, 0], z_in[b - 1, 1]))
        if b + 1 < BATCHES:
            mean_at(b, b + 1, w_parts)

    mean = 0.1 * mean_state(BATCHES - 1, xb)
    for i in range(OWN):
        m = me * OWN + i
        x = 0.8 * xb[anc_ref[BATCHES - 1, 0, m]] + 0.3 * xb[m] - mean
        out_ref[i] = x[:VARS]


def local(regions, x, observed, obs_error, obs_index, pattern, ancestors):
    whole = pl.BlockSpec(memory_space=pltpu.VMEM)
    vmem = pltpu.VMEM
    return pl.pallas_call(
        functools.partial(body, regions),
        out_shape=jax.ShapeDtypeStruct((OWN, VARS, CELLS), F32),
        in_specs=[pl.BlockSpec(memory_space=pltpu.HBM)] * 6,
        out_specs=whole,
        scratch_shapes=[
            vmem((OWN, VARS, CELLS), F32),
            vmem((BATCHES, OBS), F32),
            vmem((BATCHES, OBS), F32),
            vmem((BATCHES, OBS), jnp.int32),
            pltpu.SMEM((BATCHES, 1, 3, 2, OTILES), jnp.int32),
            pltpu.SMEM((BATCHES, 1, MEMBERS), jnp.int32),
            vmem((OWN, 16, CELLS), F32),
            vmem((2, 256, 128), F32),
            vmem((3 * 16 * VARS, CELLS), BF16),
            vmem((BATCHES, CELLS, OBS), BF16),
            vmem((BATCHES - 1, 128, 128), F32),
            vmem((BATCHES - 1, OWN, OTILES, 128), F32),
            *[vmem((8 * MEMBERS, 128), F32)] * 9,
            *[vmem((MEMBERS, OTILES, 128), F32)] * 6,
            vmem((MEMBERS, 16, CELLS), F32),
            vmem((MEMBERS, 16, CELLS), F32),
            vmem((OBS, CELLS), F32),
            vmem((OBS, CELLS), BF16),
            vmem((OBS, CELLS), BF16),
            vmem((2, OBS, 128), BF16),
            vmem((2, 2, 128, CELLS), BF16),
            vmem((16, 128), F32),
            vmem((2, 2, 16, 128), F32),
            vmem((16, CELLS), F32),
            vmem((16, CELLS), F32),
            vmem((24, CELLS), F32),
            vmem((ALONG_X, 24, CELLS), F32),
            vmem((MEMBERS, CELLS), F32),
            vmem((BATCHES - 1, MEMBERS, 128), F32),
            vmem((BATCHES - 1, 2, MEMBERS, 128), F32),
            vmem((MEMBERS, CELLS), F32),
            vmem((BATCHES, MEMBERS, CELLS), F32),
            vmem((24, 128), F32),
            vmem((16, CELLS), F32),
            pltpu.SemaphoreType.DMA((6,)),
            pltpu.SemaphoreType.DMA((56,)),
            pltpu.SemaphoreType.DMA((56,)),
        ],
        compiler_params=pltpu.CompilerParams(
            collective_id=0, has_side_effects=True, vmem_limit_bytes=56 << 20
        ),
        name="particle_filter",
    )(x, observed, obs_error, obs_index, jnp.swapaxes(pattern, 3, 4), ancestors)


def solution(mesh):
    placed = (
        P("member", None, "region"),
        P(None, "region"),
        P(None, "region"),
        P(None, "region"),
        P(None, "region", None, None, None),
        P(None, "region", None),
    )
    return jax.shard_map(
        functools.partial(local, mesh.shape["region"]),
        mesh=mesh, in_specs=placed, out_specs=P("member", None, "region"), check_vma=False,
    )
```

time: 52.3 us -> 43.3 us (0.83)
  the two profiles are of different devices: /device:TPU:2 before, /device:TPU:8 now
where the time goes in v2:
time: 43.3 us; the launch traced here: 43.2 us
  Pallas kernels  41.6 us (96%)
  local copies, waits for them, and re-layouts  1.59 us (4%)
    pallas_call x1, Pallas kernels, local(): pl.pallas_call(functools.partial(body, regions), out_shape=jax.ShapeDtype...  41.6 us
    unnamed x1, local copies, waits for them, and re-layouts  1.59 us

profile of v2, /device:TPU:8, one launch (start us, length us, event | category | flops | bytes accessed | tf_op | source)
XLA Modules:
  0.0 43.2 jit_solution(16465787938246737451)
XLA Ops:
  0.0 41.6 %particle_filter.1 = f32[10,15,256]{2,1,0:T(8,128)} custom-call(f32[10,15,256]{2,1,0:T(8,128)} %x_hbm.1, f32[4,512]{1,0:T(4,128)} %obs_hbm.1, f32[4,512]{1,0:T(4,128)} %err_hbm.1, s32[4,512]{1,0:T(4,128)} %idx_hbm.1, s32[4,1,3,2,4]{4,3,2,1,0:T(2,128)} %bitcast.1, s32[4,1,80]{2,1,0:T(1,128)} %anc_hbm.1), custom_call_target="tpu_custom_call" | custom-call | tf_op jit(solution)/shard_map/particle_filter/pallas_call | solution.py:396
  41.6 1.6 %copy.8 = f32[10,15,256]{2,1,0:T(8,128)} copy(f32[10,15,256]{2,1,0:T(8,128)} %particle_filter.1) | data formatting | bytes 307200

commit v3 on v2

--- a/solution.py
+++ b/solution.py
@@ -20,6 +20,7 @@
 OTILES = 4
 ALONG_X = 4
 Z_CHIPS, EARLY_FAR, EARLY_NEAR = 8, 4, 4
+LAST_SENDS = (0, 0)
 
 
 def split2(a):
@@ -47,7 +48,7 @@
     x_ref, obs_ref, err_ref, idx_ref, pat_ref, anc_ref,
     xs, xh, lhs, onehot, own_2d, own_h, y10, y20, y30, y11, y21, y31, y22, y32, y33,
     h1, h2, h3, h21, h31, h32, xa, xb,
-    taper, loc_hi, loc_lo, reach, land, z_own, z_first, self_own, self_far, s_out, s_in, s_all, z_out, z_in,
+    taper, loc, reach, land, z_own, z_first, self_own, self_far, s_out, s_in, s_all, z_out, z_in,
     self_scores, w_all, mean_h, mean_x,
     load_sem, send, recv,
 ):
@@ -58,7 +59,9 @@
     base = me - along_x
     near_half = me // ALONG_X
     z = (r // 2) % Z_CHIPS
-    early_far, early_near = z < EARLY_FAR, z < EARLY_NEAR
+    early_far, last = z < EARLY_FAR, z == Z_CHIPS - 1
+    middle = jnp.logical_not(jnp.logical_or(early_far, last))
+    early_near = jnp.logical_and(z < EARLY_NEAR, r % (2 * Z_CHIPS) != 0)
 
     def beside(step):
         n = r + step
@@ -93,7 +96,7 @@
     tile = lax.broadcasted_iota(jnp.int32, (OBS, 128), 1)
     away = jnp.where(tile < OTILES, at // 2, CELLS - at // 2).astype(F32)
     held_by = jnp.logical_and(tile < 2 * OTILES, tile % OTILES == at // 128)
-    reach[0], reach[1] = split2(jnp.where(held_by, jnp.exp(away * (-1.0 / (0.5 * CELLS))), 0.0))
+    reach[:, :128], reach[:, 128:] = split2(jnp.where(held_by, jnp.exp(away * (-1.0 / (0.5 * CELLS))), 0.0))
     for zeroed in (xs, xh, land):
         zeroed[...] = jnp.zeros_like(zeroed)
 
@@ -111,29 +114,28 @@
     def localize(b):
         for t in range(OTILES):
             rows = pl.ds(128 * t, 128)
-            loc_hi[rows, :], loc_lo[rows, :] = split2(taper[rows, :] * blocks(b, 1, t))
+            loc[rows, :CELLS], loc[rows, CELLS:] = split2(taper[rows, :] * blocks(b, 1, t))
         lands = []
         for k, gap in ((2, CELLS - lane), (0, lane)):
             factor = jnp.exp(gap.astype(F32) * (-1.0 / (0.5 * CELLS)))
             lands += [factor * blocks(b, k, t) for t in range(OTILES)]
         hi, lo = split2(jnp.concatenate(lands + [jnp.zeros((8, CELLS), F32)], axis=0))
-        land[b % 2, 0, pl.ds(0, 16), :], land[b % 2, 1, pl.ds(0, 16), :] = hi, lo
-
-    def product(a, b_hi, b_lo):
-        n = a.shape[0]
-        hi, lo = split2(a)
-        both = dot(jnp.concatenate([hi, lo], axis=0), b_hi)
-        return both[:n] + both[n:] + dot(hi, b_lo)
+        land[b % 2, pl.ds(0, 16), :CELLS], land[b % 2, pl.ds(0, 16), CELLS:] = hi, lo
+
+    def product(a, b):
+        n, k = a.shape[0], b.shape[1] // 2
+        all_four = dot(jnp.concatenate(split2(a), axis=0), b)
+        return all_four[:n, :k] + (all_four[n:, :k] + all_four[:n, k:]) + all_four[n:, k:]
 
     def own_scores(q):
-        return product(q, loc_hi[...], loc_lo[...])
+        return product(q, loc[...])
 
     def beside_sums(q):
-        return product(q, reach[0], reach[1])
+        return product(q, reach[...])
 
     def beside_scores(b, from_left, from_right):
         lanes = lax.broadcasted_iota(jnp.int32, from_left.shape, 1)
-        return product(jnp.where(lanes < OTILES, from_right, from_left), land[b % 2, 0], land[b % 2, 1])
+        return product(jnp.where(lanes < OTILES, from_right, from_left), land[b % 2])
 
     loads[0].wait()
     locate(0)
@@ -187,9 +189,13 @@
         for c in copies:
             c.start()
 
-    def wait(copies):
+    def arrive(copies):
         for c in copies:
-            c.wait()
+            c.wait_recv()
+
+    def leave(copies):
+        for c in copies:
+            c.wait_send()
 
     for c in loads[3:]:
         c.wait()
@@ -211,22 +217,43 @@
 
     held_h = {1: h1, 2: h2, 3: h3}
     samples = {b: gather(own_h.at[b - 1], held_h[b], 35 + 7 * (b - 1)) for b in (1, 2, 3)}
-    members = gather(xs, xa, 0)
+    mine, theirs = members_of(me), members_of(far)
+    near = [copy(xs, xa.at[mine], i, p) for i, p in enumerate(partners)]
+    halves = (pl.ds(0, 8), pl.ds(8, 8))
+    over = [copy(xs.at[:, rows], xa.at[mine, rows], 3 + i, across) for i, rows in enumerate(halves)]
+    onward = [
+        [copy(xa.at[theirs, rows], xa.at[theirs, rows], 5 + 3 * i + j, p) for j, p in enumerate(partners)]
+        for i, rows in enumerate(halves)
+    ]
+
+    def send_over(phase):
+        now = [c for c, at in zip(over, LAST_SENDS) if at == phase]
+        if now:
+            @pl.when(last)
+            def _():
+                start(now)
+
+    def pass_on(parts=(0, 1)):
+        for i in parts:
+            arrive(over[i : i + 1])
+            start(onward[i])
+
     for b in (1, 2, 3):
         locate(b)
         keep_sample(b)
         held_h[b][members_of(me)] = own_h[b - 1]
-        if b < 3:
-            samples[b][1].start()
+        samples[b][1].start()
         start(samples[b][0])
 
     @pl.when(early_far)
     def _():
-        members[1].start()
+        start(over)
 
     @pl.when(early_near)
     def _():
-        start(members[0])
+        start(near)
+
+    send_over(0)
 
     xa[members_of(me)] = xs[...]
 
@@ -297,14 +324,16 @@
         w_all[b] = weights
         return jnp.concatenate(split2(weights), axis=0)
 
-    samples[1][1].wait()
+    arrive(samples[1][1:2])
     start(samples[1][2])
-    wait(first_copies)
-    samples[3][1].start()
-
-    @pl.when(jnp.logical_not(early_far))
+
+    arrive(first_copies)
+
+    @pl.when(middle)
     def _():
-        members[1].start()
+        start(over)
+
+    send_over(1)
 
     sums = beside_scores(
         0,
@@ -318,11 +347,17 @@
     start(s_copies)
     s_in[along_x] = s_out[...]
     localize(1)
-    samples[2][1].wait()
-    start(samples[2][2])
-    wait((*samples[1][0], *samples[1][2]))
+    for b in (2, 3):
+        arrive(samples[b][1:2])
+        start(samples[b][2])
+
+    @pl.when(jnp.logical_not(early_near))
+    def _():
+        start(near)
+
+    arrive((*samples[1][0], *samples[1][2]))
     evolve(0, 1)
-    wait(s_copies)
+    arrive(s_copies)
     for half, first in ((0, near_half), (1, 1 - near_half)):
         rows = jnp.concatenate([s_in[i, pl.ds(OWN * half, OWN), :] for i in range(ALONG_X)], axis=0)
         s_all[pl.ds(pl.multiple_of(first * (MEMBERS // 2), 8), MEMBERS // 2), :] = rows
@@ -330,6 +365,9 @@
     w_parts = weigh(0, s_all[...])
     mean_at(0, 1, w_parts)
 
+    sent = [*first_copies, *s_copies]
+    for group in samples.values():
+        sent += [*group[0], group[1], *group[2]]
     for b in range(1, BATCHES):
         q = terms(b)
         z_out[b - 1] = beside_sums(q)
@@ -341,44 +379,49 @@
         self_scores[...] = own_scores(q)
 
         if b == 1:
-            samples[3][1].wait()
-            start(samples[3][2])
-
-            @pl.when(jnp.logical_not(early_near))
-            def _():
-                start(members[0])
+            send_over(2)
 
             @pl.when(early_far)
             def _():
-                members[1].wait()
-                start(members[2])
-
-            wait((*samples[2][0], *samples[2][2]))
+                pass_on()
+
+            arrive((*samples[2][0], *samples[2][2]))
             evolve(0, 2)
             mean_at(0, 2, w_parts)
             evolve(1, 2)
             held_w = w_parts
         if b == 2:
-            @pl.when(jnp.logical_not(early_far))
+            send_over(3)
+
+            @pl.when(middle)
             def _():
-                members[1].wait()
-                start(members[2])
-
-            wait((*samples[3][0], *samples[3][2]))
+                pass_on()
+
+            arrive((*samples[3][0], *samples[3][2]))
             evolve(0, 3)
             mean_at(0, 3, held_w)
             evolve(1, 3)
             mean_at(1, 3, w_parts)
             evolve(2, 3)
+
+            @pl.when(last)
+            def _():
+                pass_on([i for i in (0, 1) if LAST_SENDS[i] < 3])
         if b == 3:
-            wait((*members[0], *members[2]))
+            @pl.when(last)
+            def _():
+                pass_on([i for i in (0, 1) if LAST_SENDS[i] >= 3])
+
+            arrive((*near, *onward[0], *onward[1]))
             advance(0, xa, xb)
+            leave((*near, *over, *onward[0], *onward[1]))
             advance(1, xb, xa)
             advance(2, xa, xb)
         if b + 1 < BATCHES:
             localize(b + 1)
 
-        wait(halo)
+        arrive(halo)
+        sent += halo
         w_parts = weigh(b, self_scores[...] + beside_scores(b, z_in[b - 1, 0], z_in[b - 1, 1]))
         if b + 1 < BATCHES:
             mean_at(b, b + 1, w_parts)
@@ -388,6 +431,7 @@
         m = me * OWN + i
         x = 0.8 * xb[anc_ref[BATCHES - 1, 0, m]] + 0.3 * xb[m] - mean
         out_ref[i] = x[:VARS]
+    leave(sent)
 
 
 def local(regions, x, observed, obs_error, obs_index, pattern, ancestors):
@@ -416,10 +460,9 @@
             vmem((MEMBERS, 16, CELLS), F32),
             vmem((MEMBERS, 16, CELLS), F32),
             vmem((OBS, CELLS), F32),
-            vmem((OBS, CELLS), BF16),
-            vmem((OBS, CELLS), BF16),
-            vmem((2, OBS, 128), BF16),
-            vmem((2, 2, 128, CELLS), BF16),
+            vmem((OBS, 2 * CELLS), BF16),
+            vmem((OBS, 2 * 128), BF16),
+            vmem((2, 128, 2 * CELLS), BF16),
             vmem((16, 128), F32),
             vmem((2, 2, 16, 128), F32),
             vmem((16, CELLS), F32),

time: 43.3 us -> 41 us (0.947)
  the two profiles are of different devices: /device:TPU:8 before, /device:TPU:2 now
where the time goes in v3:
time: 41 us; the launch traced here: 40.8 us
  Pallas kernels  39.2 us (96%)
  local copies, waits for them, and re-layouts  1.59 us (4%)
    pallas_call x1, Pallas kernels, local(): pl.pallas_call(functools.partial(body, regions), out_shape=jax.ShapeDtype...  39.2 us
    unnamed x1, local copies, waits for them, and re-layouts  1.59 us

profile of v3, /device:TPU:2, one launch (start us, length us, event | category | flops | bytes accessed | tf_op | source)
XLA Modules:
  0.0 40.8 jit_solution(2083938384176179981)
XLA Ops:
  0.0 39.2 %particle_filter.1 = f32[10,15,256]{2,1,0:T(8,128)} custom-call(f32[10,15,256]{2,1,0:T(8,128)} %x_hbm.1, f32[4,512]{1,0:T(4,128)} %obs_hbm.1, f32[4,512]{1,0:T(4,128)} %err_hbm.1, s32[4,512]{1,0:T(4,128)} %idx_hbm.1, s32[4,1,3,2,4]{4,3,2,1,0:T(2,128)} %bitcast.1, s32[4,1,80]{2,1,0:T(1,128)} %anc_hbm.1), custom_call_target="tpu_custom_call" | custom-call | tf_op jit(solution)/shard_map/particle_filter/pallas_call | solution.py:440
  39.2 1.6 %copy.8 = f32[10,15,256]{2,1,0:T(8,128)} copy(f32[10,15,256]{2,1,0:T(8,128)} %particle_filter.1) | data formatting | bytes 307200

commit v4 on v3

--- a/solution.py
+++ b/solution.py
@@ -20,7 +20,7 @@
 OTILES = 4
 ALONG_X = 4
 Z_CHIPS, EARLY_FAR, EARLY_NEAR = 8, 4, 4
-LAST_SENDS = (0, 0)
+PARTS = 4
 
 
 def split2(a):
@@ -60,7 +60,7 @@
     near_half = me // ALONG_X
     z = (r // 2) % Z_CHIPS
     early_far, last = z < EARLY_FAR, z == Z_CHIPS - 1
-    middle = jnp.logical_not(jnp.logical_or(early_far, last))
+    middle = z < 0
     early_near = jnp.logical_and(z < EARLY_NEAR, r % (2 * Z_CHIPS) != 0)
 
     def beside(step):
@@ -97,7 +97,7 @@
     away = jnp.where(tile < OTILES, at // 2, CELLS - at // 2).astype(F32)
     held_by = jnp.logical_and(tile < 2 * OTILES, tile % OTILES == at // 128)
     reach[:, :128], reach[:, 128:] = split2(jnp.where(held_by, jnp.exp(away * (-1.0 / (0.5 * CELLS))), 0.0))
-    for zeroed in (xs, xh, land):
+    for zeroed in (xs, xh):
         zeroed[...] = jnp.zeros_like(zeroed)
 
     def locate(b):
@@ -119,8 +119,7 @@
         for k, gap in ((2, CELLS - lane), (0, lane)):
             factor = jnp.exp(gap.astype(F32) * (-1.0 / (0.5 * CELLS)))
             lands += [factor * blocks(b, k, t) for t in range(OTILES)]
-        hi, lo = split2(jnp.concatenate(lands + [jnp.zeros((8, CELLS), F32)], axis=0))
-        land[b % 2, pl.ds(0, 16), :CELLS], land[b % 2, pl.ds(0, 16), CELLS:] = hi, lo
+        land[b % 2] = jnp.concatenate(lands, axis=0)
 
     def product(a, b):
         n, k = a.shape[0], b.shape[1] // 2
@@ -133,9 +132,12 @@
     def beside_sums(q):
         return product(q, reach[...])
 
-    def beside_scores(b, from_left, from_right):
-        lanes = lax.broadcasted_iota(jnp.int32, from_left.shape, 1)
-        return product(jnp.where(lanes < OTILES, from_right, from_left), land[b % 2])
+    def beside_scores(b, from_left, from_right, start):
+        total = start
+        for i in range(2 * OTILES):
+            sums = (from_right if i < OTILES else from_left)[:, i : i + 1]
+            total = total + sums * land[b % 2, pl.ds(i, 1), :]
+        return total
 
     loads[0].wait()
     locate(0)
@@ -217,27 +219,7 @@
 
     held_h = {1: h1, 2: h2, 3: h3}
     samples = {b: gather(own_h.at[b - 1], held_h[b], 35 + 7 * (b - 1)) for b in (1, 2, 3)}
-    mine, theirs = members_of(me), members_of(far)
-    near = [copy(xs, xa.at[mine], i, p) for i, p in enumerate(partners)]
-    halves = (pl.ds(0, 8), pl.ds(8, 8))
-    over = [copy(xs.at[:, rows], xa.at[mine, rows], 3 + i, across) for i, rows in enumerate(halves)]
-    onward = [
-        [copy(xa.at[theirs, rows], xa.at[theirs, rows], 5 + 3 * i + j, p) for j, p in enumerate(partners)]
-        for i, rows in enumerate(halves)
-    ]
-
-    def send_over(phase):
-        now = [c for c, at in zip(over, LAST_SENDS) if at == phase]
-        if now:
-            @pl.when(last)
-            def _():
-                start(now)
-
-    def pass_on(parts=(0, 1)):
-        for i in parts:
-            arrive(over[i : i + 1])
-            start(onward[i])
-
+    near, over, onward = gather(xs, xa, 0)
     for b in (1, 2, 3):
         locate(b)
         keep_sample(b)
@@ -245,15 +227,14 @@
         samples[b][1].start()
         start(samples[b][0])
 
-    @pl.when(early_far)
+    @pl.when(jnp.logical_not(middle))
     def _():
-        start(over)
+        over.start()
 
     @pl.when(early_near)
     def _():
         start(near)
 
-    send_over(0)
 
     xa[members_of(me)] = xs[...]
 
@@ -303,11 +284,12 @@
             mean_h[mean_row(batch, t), :] = m
 
     def mean_state(b, x):
-        def step(m, acc):
-            w = w_all[b, pl.ds(m, 1), :]
-            return acc + w * x[m]
-
-        return lax.fori_loop(0, MEMBERS, step, jnp.zeros((16, CELLS), F32), unroll=8)
+        def step(i, parts):
+            at = [PARTS * i + j for j in range(PARTS)]
+            return tuple(part + w_all[b, pl.ds(m, 1), :] * x[m] for part, m in zip(parts, at))
+
+        parts = lax.fori_loop(0, MEMBERS // PARTS, step, (jnp.zeros((16, CELLS), F32),) * PARTS, unroll=4)
+        return (parts[0] + parts[1]) + (parts[2] + parts[3])
 
     def advance(b, x, y):
         mean_x[...] = 0.1 * mean_state(b, x)
@@ -331,17 +313,13 @@
 
     @pl.when(middle)
     def _():
-        start(over)
-
-    send_over(1)
-
-    sums = beside_scores(
-        0,
-        jnp.concatenate([z_first[0, 0], z_first[0, 1]], axis=0),
-        jnp.concatenate([z_first[1, 0], z_first[1, 1]], axis=0),
+        over.start()
+
+    near_scores, far_scores = (
+        beside_scores(0, z_first[0, i], z_first[1, i], own[...]) for i, own in enumerate((self_own, self_far))
     )
-    s_out[pl.ds(0, 16), :] = sums[:16] + self_own[...]
-    s_out[pl.ds(OWN, OWN), :] = (sums[16:] + self_far[...])[:OWN]
+    s_out[pl.ds(0, 16), :] = near_scores
+    s_out[pl.ds(OWN, OWN), :] = far_scores[:OWN]
     s_out[pl.ds(2 * OWN, 4), :] = jnp.zeros((4, CELLS), F32)
     s_copies = [copy(s_out, s_in.at[along_x], 26 + i, p) for i, p in enumerate(partners)]
     start(s_copies)
@@ -351,13 +329,13 @@
         arrive(samples[b][1:2])
         start(samples[b][2])
 
+    arrive((*samples[1][0], *samples[1][2]))
+    evolve(0, 1)
+    arrive(s_copies)
     @pl.when(jnp.logical_not(early_near))
     def _():
         start(near)
 
-    arrive((*samples[1][0], *samples[1][2]))
-    evolve(0, 1)
-    arrive(s_copies)
     for half, first in ((0, near_half), (1, 1 - near_half)):
         rows = jnp.concatenate([s_in[i, pl.ds(OWN * half, OWN), :] for i in range(ALONG_X)], axis=0)
         s_all[pl.ds(pl.multiple_of(first * (MEMBERS // 2), 8), MEMBERS // 2), :] = rows
@@ -379,23 +357,26 @@
         self_scores[...] = own_scores(q)
 
         if b == 1:
-            send_over(2)
-
             @pl.when(early_far)
             def _():
-                pass_on()
+                over.wait_recv()
+                start(onward)
 
             arrive((*samples[2][0], *samples[2][2]))
             evolve(0, 2)
             mean_at(0, 2, w_parts)
             evolve(1, 2)
             held_w = w_parts
+
+            @pl.when(jnp.logical_not(early_far))
+            def _():
+                over.wait_recv()
+                start(onward)
         if b == 2:
-            send_over(3)
-
             @pl.when(middle)
             def _():
-                pass_on()
+                over.wait_recv()
+                start(onward)
 
             arrive((*samples[3][0], *samples[3][2]))
             evolve(0, 3)
@@ -403,34 +384,27 @@
             evolve(1, 3)
             mean_at(1, 3, w_parts)
             evolve(2, 3)
-
-            @pl.when(last)
-            def _():
-                pass_on([i for i in (0, 1) if LAST_SENDS[i] < 3])
         if b == 3:
-            @pl.when(last)
-            def _():
-                pass_on([i for i in (0, 1) if LAST_SENDS[i] >= 3])
-
-            arrive((*near, *onward[0], *onward[1]))
+            arrive((*near, *onward))
             advance(0, xa, xb)
-            leave((*near, *over, *onward[0], *onward[1]))
+            leave((*near, over, *onward))
             advance(1, xb, xa)
             advance(2, xa, xb)
+            for i in range(OWN):
+                m = me * OWN + i
+                xs[i] = 0.8 * xb[anc_ref[b, 0, m]] + 0.3 * xb[m]
         if b + 1 < BATCHES:
             localize(b + 1)
 
         arrive(halo)
         sent += halo
-        w_parts = weigh(b, self_scores[...] + beside_scores(b, z_in[b - 1, 0], z_in[b - 1, 1]))
+        w_parts = weigh(b, beside_scores(b, z_in[b - 1, 0], z_in[b - 1, 1], self_scores[...]))
         if b + 1 < BATCHES:
             mean_at(b, b + 1, w_parts)
 
     mean = 0.1 * mean_state(BATCHES - 1, xb)
     for i in range(OWN):
-        m = me * OWN + i
-        x = 0.8 * xb[anc_ref[BATCHES - 1, 0, m]] + 0.3 * xb[m] - mean
-        out_ref[i] = x[:VARS]
+        out_ref[i] = xs[i, pl.ds(0, VARS), :] - mean[:VARS]
     leave(sent)
 
 
@@ -462,7 +436,7 @@
             vmem((OBS, CELLS), F32),
             vmem((OBS, 2 * CELLS), BF16),
             vmem((OBS, 2 * 128), BF16),
-            vmem((2, 128, 2 * CELLS), BF16),
+            vmem((2, 2 * OTILES, CELLS), F32),
             vmem((16, 128), F32),
             vmem((2, 2, 16, 128), F32),
             vmem((16, CELLS), F32),

time: 41 us -> 40.9 us (level)
  no operation moved by 1% of the time
where the time goes in v4:
time: 40.9 us; the launch traced here: 40.7 us
  Pallas kernels  39.1 us (96%)
  local copies, waits for them, and re-layouts  1.59 us (4%)
    pallas_call x1, Pallas kernels, local(): pl.pallas_call(functools.partial(body, regions), out_shape=jax.ShapeDtype...  39.1 us
    unnamed x1, local copies, waits for them, and re-layouts  1.59 us

profile of v4, /device:TPU:2, one launch (start us, length us, event | category | flops | bytes accessed | tf_op | source)
XLA Modules:
  0.0 40.7 jit_solution(4123691482214563157)
XLA Ops:
  0.0 39.1 %particle_filter.1 = f32[10,15,256]{2,1,0:T(8,128)} custom-call(f32[10,15,256]{2,1,0:T(8,128)} %x_hbm.1, f32[4,512]{1,0:T(4,128)} %obs_hbm.1, f32[4,512]{1,0:T(4,128)} %err_hbm.1, s32[4,512]{1,0:T(4,128)} %idx_hbm.1, s32[4,1,3,2,4]{4,3,2,1,0:T(2,128)} %bitcast.1, s32[4,1,80]{2,1,0:T(1,128)} %anc_hbm.1), custom_call_target="tpu_custom_call" | custom-call | tf_op jit(solution)/shard_map/particle_filter/pallas_call | solution.py:414
  39.1 1.6 %copy.8 = f32[10,15,256]{2,1,0:T(8,128)} copy(f32[10,15,256]{2,1,0:T(8,128)} %particle_filter.1) | data formatting | bytes 307200

commit v5 on v4

--- a/solution.py
+++ b/solution.py
@@ -93,9 +93,9 @@
     column = lax.broadcasted_iota(jnp.int32, (OBS, CELLS), 1)
     taper[...] = jnp.exp(jnp.abs(at - column).astype(F32) * (-1.0 / (0.5 * CELLS)))
     at = lax.broadcasted_iota(jnp.int32, (OBS, 128), 0)
-    tile = lax.broadcasted_iota(jnp.int32, (OBS, 128), 1)
+    tile = lax.broadcasted_iota(jnp.int32, (OBS, 128), 1) % (2 * OTILES)
     away = jnp.where(tile < OTILES, at // 2, CELLS - at // 2).astype(F32)
-    held_by = jnp.logical_and(tile < 2 * OTILES, tile % OTILES == at // 128)
+    held_by = tile % OTILES == at // 128
     reach[:, :128], reach[:, 128:] = split2(jnp.where(held_by, jnp.exp(away * (-1.0 / (0.5 * CELLS))), 0.0))
     for zeroed in (xs, xh):
         zeroed[...] = jnp.zeros_like(zeroed)
@@ -130,14 +130,22 @@
         return product(q, loc[...])
 
     def beside_sums(q):
-        return product(q, reach[...])
+        sums = product(q, reach[...])
+        held = lax.broadcasted_iota(jnp.int32, (8, 128), 1) // 8
+        packed = jnp.zeros((8, 128), F32)
+        for g in range(q.shape[0] // 8):
+            packed = jnp.where(held == g, sums[8 * g : 8 * g + 8], packed)
+        return packed
 
     def beside_scores(b, from_left, from_right, start):
-        total = start
-        for i in range(2 * OTILES):
-            sums = (from_right if i < OTILES else from_left)[:, i : i + 1]
-            total = total + sums * land[b % 2, pl.ds(i, 1), :]
-        return total
+        found = []
+        for g in range(start.shape[0] // 8):
+            total = start[8 * g : 8 * g + 8]
+            for i in range(2 * OTILES):
+                sums = (from_right if i < OTILES else from_left)[:, 8 * g + i : 8 * g + i + 1]
+                total = total + sums * land[b % 2, pl.ds(i, 1), :]
+            found.append(total)
+        return jnp.concatenate(found, axis=0)
 
     loads[0].wait()
     locate(0)
@@ -437,15 +445,15 @@
             vmem((OBS, 2 * CELLS), BF16),
             vmem((OBS, 2 * 128), BF16),
             vmem((2, 2 * OTILES, CELLS), F32),
-            vmem((16, 128), F32),
-            vmem((2, 2, 16, 128), F32),
+            vmem((8, 128), F32),
+            vmem((2, 2, 8, 128), F32),
             vmem((16, CELLS), F32),
             vmem((16, CELLS), F32),
             vmem((24, CELLS), F32),
             vmem((ALONG_X, 24, CELLS), F32),
             vmem((MEMBERS, CELLS), F32),
-            vmem((BATCHES - 1, MEMBERS, 128), F32),
-            vmem((BATCHES - 1, 2, MEMBERS, 128), F32),
+            vmem((BATCHES - 1, 8, 128), F32),
+            vmem((BATCHES - 1, 2, 8, 128), F32),
             vmem((MEMBERS, CELLS), F32),
             vmem((BATCHES, MEMBERS, CELLS), F32),
             vmem((24, 128), F32),

time: 40.9 us -> 40.3 us (0.985)
  the two profiles are of different devices: /device:TPU:2 before, /device:TPU:8 now
where the time goes in v5:
time: 40.3 us; the launch traced here: 40.1 us
  Pallas kernels  38.5 us (96%)
  local copies, waits for them, and re-layouts  1.59 us (4%)
    pallas_call x1, Pallas kernels, local(): pl.pallas_call(functools.partial(body, regions), out_shape=jax.ShapeDtype...  38.5 us
    unnamed x1, local copies, waits for them, and re-layouts  1.59 us

profile of v5, /device:TPU:8, one launch (start us, length us, event | category | flops | bytes accessed | tf_op | source)
XLA Modules:
  0.0 40.1 jit_solution(4972226556846658840)
XLA Ops:
  0.0 38.5 %particle_filter.1 = f32[10,15,256]{2,1,0:T(8,128)} custom-call(f32[10,15,256]{2,1,0:T(8,128)} %x_hbm.1, f32[4,512]{1,0:T(4,128)} %obs_hbm.1, f32[4,512]{1,0:T(4,128)} %err_hbm.1, s32[4,512]{1,0:T(4,128)} %idx_hbm.1, s32[4,1,3,2,4]{4,3,2,1,0:T(2,128)} %bitcast.1, s32[4,1,80]{2,1,0:T(1,128)} %anc_hbm.1), custom_call_target="tpu_custom_call" | custom-call | tf_op jit(solution)/shard_map/particle_filter/pallas_call | solution.py:422
  38.5 1.6 %copy.8 = f32[10,15,256]{2,1,0:T(8,128)} copy(f32[10,15,256]{2,1,0:T(8,128)} %particle_filter.1) | data formatting | bytes 307200

commit v6 on v5

--- a/solution.py
+++ b/solution.py
@@ -103,7 +103,8 @@
     def locate(b):
         where = idx_ref[pl.ds(b, 1), :]
         rows = lax.broadcasted_iota(jnp.int32, (CELLS, OBS), 0)
-        onehot[b] = jnp.where(rows == where % CELLS, 1.0, 0.0).astype(BF16)
+        hot = jnp.where(rows == where % CELLS, 1.0, 0.0).astype(BF16)
+        onehot[b, :CELLS], onehot[b, CELLS:] = hot, hot
 
     lane = lax.broadcasted_iota(jnp.int32, (1, CELLS), 1)
 
@@ -164,7 +165,7 @@
 
     def sample(b):
         var = idx_ref[pl.ds(b, 1), :] // CELLS
-        got = dot(lhs[...], onehot[b])
+        got = dot(lhs[...], onehot[b, :CELLS])
         n = 16 * VARS
         got = got[:n] + got[n : 2 * n] + got[2 * n :]
         total = jnp.zeros((16, OBS), F32)
@@ -284,7 +285,6 @@
 
     def mean_at(b, batch, w_parts):
         wm = dot(w_parts, onehot[batch])
-        wm = wm[:MEMBERS] + wm[MEMBERS:]
         for t, y in enumerate(rows_at(b, batch)):
             m = jnp.sum(wm[:, 128 * t : 128 * t + 128] * y, axis=0, keepdims=True)
             if b > 0:
@@ -312,7 +312,7 @@
         raised = jnp.exp(scores - jnp.max(scores, axis=0, keepdims=True))
         weights = raised / jnp.sum(raised, axis=0, keepdims=True)
         w_all[b] = weights
-        return jnp.concatenate(split2(weights), axis=0)
+        return jnp.concatenate(split2(weights), axis=1)
 
     arrive(samples[1][1:2])
     start(samples[1][2])
@@ -434,7 +434,7 @@
             vmem((OWN, 16, CELLS), F32),
             vmem((2, 256, 128), F32),
             vmem((3 * 16 * VARS, CELLS), BF16),
-            vmem((BATCHES, CELLS, OBS), BF16),
+            vmem((BATCHES, 2 * CELLS, OBS), BF16),
             vmem((BATCHES - 1, 128, 128), F32),
             vmem((BATCHES - 1, OWN, OTILES, 128), F32),
             *[vmem((8 * MEMBERS, 128), F32)] * 9,

time: 40.3 us -> 40.3 us (level)
  no operation moved by 1% of the time
where the time goes in v6:
time: 40.3 us; the launch traced here: 40.1 us
  Pallas kernels  38.5 us (96%)
  local copies, waits for them, and re-layouts  1.59 us (4%)
    pallas_call x1, Pallas kernels, local(): pl.pallas_call(functools.partial(body, regions), out_shape=jax.ShapeDtype...  38.5 us
    unnamed x1, local copies, waits for them, and re-layouts  1.59 us

profile of v6, /device:TPU:8, one launch (start us, length us, event | category | flops | bytes accessed | tf_op | source)
XLA Modules:
  0.0 40.1 jit_solution(16334904907298901965)
XLA Ops:
  0.0 38.5 %particle_filter.1 = f32[10,15,256]{2,1,0:T(8,128)} custom-call(f32[10,15,256]{2,1,0:T(8,128)} %x_hbm.1, f32[4,512]{1,0:T(4,128)} %obs_hbm.1, f32[4,512]{1,0:T(4,128)} %err_hbm.1, s32[4,512]{1,0:T(4,128)} %idx_hbm.1, s32[4,1,3,2,4]{4,3,2,1,0:T(2,128)} %bitcast.1, s32[4,1,80]{2,1,0:T(1,128)} %anc_hbm.1), custom_call_target="tpu_custom_call" | custom-call | tf_op jit(solution)/shard_map/particle_filter/pallas_call | solution.py:422
  38.5 1.6 %copy.8 = f32[10,15,256]{2,1,0:T(8,128)} copy(f32[10,15,256]{2,1,0:T(8,128)} %particle_filter.1) | data formatting | bytes 307200
